TPU v7x, 512 devices: a whole 4x8x8 slice. The times are simulated.
512 devices in a mesh: rep: 32 (over z, x), fsdp: 16 (over y, core).
Axes of the slice: x: 4, y: 8, z: 8, core: 2. Of those that a mesh axis runs over, the one named last changes fastest.
Arguments:
- grad_parts: bfloat16 [32, 16, 256, 6144], P('rep', 'fsdp'), may hold values from -5 to 5
- momentum: float32 [32, 256, 6144], P('rep', None, 'fsdp'), may hold values from -6 to 6
- keep_counts: int32 [32, 4, 96], P('rep', None, 'fsdp'), may hold values from 1 to 16, as said below
- keep_blocks: int32 [32, 4, 96, 16], P('rep', None, 'fsdp'), may hold values from 0 to 63, as said below
Outputs:
- update: float32 [256, 6144], P(None, 'fsdp')
- new_momentum: float32 [32, 256, 6144], P('rep', None, 'fsdp')
Inputs may be any that keep to these rules, and one draw needn't show every extreme that they name: `keep_counts`: every replica has a span that keeps exactly 16 blocks. `keep_blocks`: in each span the 16 entries are distinct block numbers; only the first keep_counts of them are kept.
All inputs are finite; a program needn't handle non-finite values.
Results may differ from a plain program's by a relative error of at most 0.0003.
Values sent between devices are 32-bit elements; how exact they have to be, the bound alone decides.
A program may use at most 64 MiB of HBM per device.

v0:
```python
import jax
import jax.numpy as jnp
from jax import lax
from jax.sharding import PartitionSpec as P

SPAN = 64
GRID = 8
KMAX = 16


def dct_table():
    frequency = jnp.arange(SPAN, dtype=jnp.float32)[:, None]
    position = jnp.arange(SPAN, dtype=jnp.float32)[None, :]
    basis = jnp.cos(jnp.pi * (2.0 * position + 1.0) * frequency / (2.0 * SPAN)) * jnp.sqrt(
        2.0 / SPAN
    )
    first_scale = jnp.where(frequency == 0.0, jnp.sqrt(0.5), 1.0)
    return basis * first_scale


def block_choice(counts, block_ids):
    slot_ids = jnp.arange(KMAX, dtype=jnp.int32)
    live_slots = slot_ids[None, None, :] < counts[:, :, None]
    numbers = jnp.arange(GRID * GRID, dtype=jnp.int32)
    return ((block_ids[:, :, :, None] == numbers) & live_slots[:, :, :, None]).astype(jnp.float32)


def shards(grad_parts, momentum, keep_counts, keep_blocks):
    rep_count = lax.axis_size("rep")
    highest = lax.Precision.HIGHEST
    basis = dct_table()
    local_grad = grad_parts[0, 0].astype(jnp.float32)
    summed = lax.psum_scatter(local_grad, "fsdp", scatter_dimension=1, tiled=True)
    fresh_moment = 0.9 * momentum[0] + summed
    row_count, col_count = fresh_moment.shape
    span_rows = row_count // SPAN
    span_cols = col_count // SPAN
    block_side = SPAN // GRID
    row_basis = jnp.kron(jnp.eye(span_rows, dtype=jnp.float32), basis)
    col_basis = jnp.kron(jnp.eye(span_cols, dtype=jnp.float32), basis)

    def inverse(values):
        inner = jnp.dot(row_basis.T, values, precision=highest, preferred_element_type=jnp.float32)
        return jnp.dot(inner, col_basis, precision=highest, preferred_element_type=jnp.float32)

    inner = jnp.dot(row_basis, fresh_moment, precision=highest, preferred_element_type=jnp.float32)
    coefficients = jnp.dot(
        inner, col_basis.T, precision=highest, preferred_element_type=jnp.float32
    )
    one_hot = block_choice(keep_counts[0], keep_blocks[0])
    chosen = one_hot.sum(axis=2).reshape(span_rows, span_cols, GRID, GRID)
    chosen = jnp.repeat(jnp.repeat(chosen, block_side, axis=2), block_side, axis=3)
    keep_field = chosen.transpose(0, 2, 1, 3).reshape(row_count, col_count)
    kept_coeff = coefficients * keep_field
    residual = fresh_moment - inverse(kept_coeff)
    grouped = kept_coeff.reshape(span_rows, GRID, block_side, span_cols, GRID, block_side)
    grouped = grouped.transpose(0, 3, 1, 4, 2, 5).reshape(
        span_rows, span_cols, GRID * GRID, block_side * block_side
    )
    packed = jnp.einsum("rckb,rcbq->rckq", one_hot, grouped, precision=highest)
    numbers = jnp.arange(GRID * GRID, dtype=jnp.int32)
    values = lax.all_gather(packed[None], "rep", axis=0, tiled=True)
    places = lax.all_gather(keep_blocks, "rep", axis=0, tiled=True)
    picks = (places[..., None] == numbers).astype(jnp.float32)
    gathered = jnp.einsum("nrckb,nrckq->rcbq", picks, values, precision=highest)
    gathered = gathered.reshape(span_rows, span_cols, GRID, GRID, block_side, block_side)
    summed_coeff = gathered.transpose(0, 2, 4, 1, 3, 5).reshape(row_count, col_count)
    update = inverse(summed_coeff / rep_count)
    return (update, residual[None])


def solution(mesh):
    return jax.shard_map(
        shards,
        mesh=mesh,
        in_specs=(
            P("rep", "fsdp", None, None),
            P("rep", None, "fsdp"),
            P("rep", None, "fsdp"),
            P("rep", None, "fsdp", None),
        ),
        out_specs=(P(None, "fsdp"), P("rep", None, "fsdp")),
        check_vma=False,
    )
```

profile of v0, /device:TPU:1, one launch (start us, length us, event | category | flops | bytes accessed | tf_op | source)
XLA Modules:
  0.0 237.0 jit_solution(15968526049429483703)
XLA Ops:
  7.2 0.0 copy-start.2
  7.2 0.0 copy-start.3
  7.2 0.0 reduce-scatter.2.cloned.1.call-start
  7.2 5.3 %bitcast_convert_fusion = f32[256,6144]{1,0:T(8,128)} fusion(bf16[1,1,256,6144]{3,2,1,0:T(8,128)(2,1)} %param.4), kind=kLoop, calls=%fused_computation.4 | loop fusion | flops 1572864 | bytes 9437184 | tf_op jit(solution)/shard_map/convert_element_type | solution.py:32
  12.5 0.0 reduce-scatter.2.cloned.1.call-update
  12.5 0.0 copy-start
  12.6 0.0 all-gather.3.cloned.1.call-start
  12.6 0.0 copy-done.2
  12.6 0.0 copy-done.3
  12.6 0.1 iota_compare_fusion.7
  12.7 0.2 convert_reduce_fusion
  12.9 0.1 reshape.130
  13.0 0.1 copy.29
  13.1 0.1 cosine_multiply_fusion
  13.2 0.1 broadcast_multiply_fusion.1
  13.4 0.3 mul.250
  13.7 0.3 broadcast_in_dim.34
  14.0 0.2 reshape.122
  14.3 0.1 broadcast_bitcast_fusion
  14.3 0.4 copy.38
  14.7 0.2 reshape.131
  15.0 0.2 broadcast_multiply_fusion
  15.2 0.4 mul.257
  15.5 69.5 %reduce-scatter.2.cloned.1.call-done = f32[256,384]{1,0:T(8,128)} async-done(((f32[256,6144]{1,0:T(8,128)}), f32[256,384]{1,0:T(8,128)}) %reduce-scatter.2.cloned.1.call-update) | async-done | bytes 393232 | tf_op jit(solution)/shard_map/reduce_scatter | solution.py:33
  85.0 0.0 copy-done
  85.0 1.6 fusion.13
  86.6 0.9 convolution_multiply_fusion
  87.6 5.1 %reshape.125 = f32[4,8,8,6,8,8]{5,4,3,2,1,0:T(8,128)} reshape(f32[256,384]{1,0:T(8,128)S(1)} %convolution_multiply_fusion) | data formatting | bytes 786432 | tf_op jit(solution)/shard_map/reshape | solution.py:56
  92.7 7.4 %copy.32 = f32[4,6,8,8,8,8]{5,4,3,2,1,0:T(8,128)} copy(f32[4,6,8,8,8,8]{5,3,1,4,2,0:T(8,128)} %bitcast.49) | data formatting | bytes 786432 | tf_op jit(solution)/shard_map/transpose | solution.py:57
  100.0 0.0 copy-start.1
  100.0 4.4 %reshape.126 = f32[4,6,64,64]{3,2,1,0:T(8,128)S(1)} reshape(f32[4,6,8,8,8,8]{5,4,3,2,1,0:T(8,128)} %copy.32) | data formatting | bytes 786432 | tf_op jit(solution)/shard_map/reshape | solution.py:57
  104.4 1.2 fusion.11
  105.6 0.0 all-gather.3.cloned.1.call-update
  105.6 39.3 %all_gather.6 = s32[32,4,6,16]{3,1,2,0:T(4,128)S(1)} all-gather(s32[1,4,6,16]{3,1,2,0:T(4,128)S(1)} %copy-done.2), channel_id=1, replica_groups=mesh['rep'=32,'fsdp'=16] {'rep'}, dimensions={0}, use_global_device_ids=true | all-gather | bytes 50688 | tf_op jit(solution)/shard_map/all_gather | solution.py:63
  144.9 0.2 copy.26
  145.1 0.6 fusion.22
  145.8 0.0 copy-done.1
  145.8 1.6 fusion.9
  147.4 54.2 %all-gather.3.cloned.1.call-done = f32[128,6,16,64]{3,2,1,0:T(8,128)} async-done(((f32[4,6,16,64]{3,2,1,0:T(8,128)}), f32[128,6,16,64]{3,2,1,0:T(8,128)}) %all-gather.3.cloned.1.call-update) | async-done | bytes 3145744 | tf_op jit(solution)/shard_map/all_gather | solution.py:62
  201.6 10.7 %fusion.6 = f32[4,6,64,64]{3,2,1,0:T(8,128)S(1)} fusion(f32[32,4,6,16,64]{4,3,2,1,0:T(8,128)} %bitcast.52, s32[32,4,6,16]{0,3,2,1:T(8,128)S(1)} %copy.26), kind=kOutput, calls=%fused_computation.7 | convolution fusion | flops 604864512 | bytes 3588096 | tf_op jit(solution)/shard_map/nrckb,nrckq->rcbq/dot_general | solution.py:65
  212.2 3.9 %div.32 = f32[4,6,8,8,8,8]{5,4,3,2,1,0:T(8,128)} reshape(f32[4,6,64,64]{3,2,1,0:T(8,128)S(1)} %fusion.6) | data formatting | bytes 786432 | tf_op jit(solution)/shard_map/div | solution.py:68
  216.1 6.6 %copy.47 = f32[4,6,8,8,8,8]{5,3,1,4,2,0:T(8,128)} copy(f32[4,6,8,8,8,8]{5,4,3,2,1,0:T(8,128)} %div.32) | data formatting | bytes 786432 | tf_op jit(solution)/shard_map/div | solution.py:68
  222.7 5.2 %div.34 = f32[256,384]{1,0:T(8,128)S(1)} reshape(f32[4,8,8,6,8,8]{5,4,3,2,1,0:T(8,128)} %bitcast.48) | data formatting | bytes 786432 | tf_op jit(solution)/shard_map/div | solution.py:68
  227.8 0.6 fusion.20
  228.5 1.6 fusion.21
  (4 shorter events, 0.0 us)
Async XLA Ops:
  7.2 5.4 %copy-start.2 = (s32[1,4,6,16]{3,1,2,0:T(4,128)S(1)}, s32[1,4,6,16]{3,1,2,0:T(4,128)}, u32[]{:S(2)}) copy-start(s32[1,4,6,16]{3,1,2,0:T(4,128)} %param.7) | copy-start | bytes 4612
  7.2 5.5 %copy-start.3 = (s32[1,4,6]{2,1,0:T(4,128)S(1)}, s32[1,4,6]{2,1,0:T(4,128)}, u32[]{:S(2)}) copy-start(s32[1,4,6]{2,1,0:T(4,128)} %param.6) | copy-start | bytes 292
  7.2 77.8 %reduce-scatter.2.cloned.1.call-start = ((), (), s32[]{:S(2)}) async-start(), calls=%async_computation.1 | async-start | bytes 6684672 | tf_op jit(solution)/shard_map/reduce_scatter | solution.py:33
  12.5 72.5 %copy-start = (f32[1,256,384]{2,1,0:T(8,128)S(1)}, f32[1,256,384]{2,1,0:T(8,128)}, u32[]{:S(2)}) copy-start(f32[1,256,384]{2,1,0:T(8,128)} %param.5) | copy-start | bytes 1179652
  12.6 189.0 %all-gather.3.cloned.1.call-start = ((), (), s32[]{:S(2)}) async-start(), calls=%async_computation.2 | async-start | bytes 6488064 | tf_op jit(solution)/shard_map/all_gather | solution.py:62
  100.0 45.7 %copy-start.1 = (f32[256,384]{1,0:T(8,128)S(1)}, f32[256,384]{1,0:T(8,128)}, u32[]{:S(2)}) copy-start(f32[256,384]{1,0:T(8,128)} %reduce-scatter.2.cloned.1.call-done) | copy-start | bytes 1179652
Sparse Core Ops, SparseCore 0:
  12.7 72.3 reduce-scatter.1
  105.7 95.7 all-gather.2
where the time goes:
time: 237 us
  waiting for transfers between devices  124 us (52%)
  blocking collectives  39.3 us (17%)
  local copies, waits for them, and re-layouts  34.7 us (15%)
  matrix products  18.9 us (8%)
  between operations  14.2 us (6%)
  other arithmetic  6.01 us (3%)
    reduce_scatter x1, waiting for transfers between devices, shards(): lax.psum_scatter(local_grad, 'fsdp', scatter_dimension=1, tiled=True)  69.5 us
    all_gather x1, waiting for transfers between devices, shards(): values = lax.all_gather(packed[None], 'rep', axis=0, tiled=True)  54.2 us
    all_gather x1, blocking collectives, shards(): places = lax.all_gather(keep_blocks, 'rep', axis=0, tiled=True)  39.3 us
    div x3, local copies, waits for them, and re-layouts, shards(): update = inverse(summed_coeff / rep_count)  15.6 us
    dot_general x1, matrix products, shards(): gathered = jnp.einsum('nrckb,nrckq->rcbq', picks, values, precision=highest)  10.7 us
    transpose x1, local copies, waits for them, and re-layouts, shards(): grouped.transpose(0, 3, 1, 4, 2, 5)  7.35 us
    convert_element_type x1, other arithmetic, shards(): local_grad = grad_parts[0, 0].astype(jnp.float32)  5.28 us
    reshape x1, local copies, waits for them, and re-layouts, shards(): kept_coeff.reshape(span_rows, GRID, block_side, span_cols, GRID, block_side)  5.1 us
  transfers between devices with their start and end apart: 2, of which 2 were waited for; matrix products, arithmetic and copies ran while one was open for 2% of the time, Pallas kernels for 0%

commit v1 on v0

v1 whole, which is shorter than its diff:
```python
import functools

import jax
import jax.numpy as jnp
import numpy as np
from jax import lax
from jax.experimental import pallas as pl
from jax.experimental.pallas import tpu as pltpu
from jax.sharding import PartitionSpec as P

MESH = pl.DeviceIdType.MESH
F32 = jnp.float32
BF16 = jnp.bfloat16

SPAN = 64
GRID = 8
KMAX = 16
NZ, NX, NY, NCORE = 8, 4, 8, 2
ROWS, COLS, WIDE = 256, 384, 6144
CHUNKS = ROWS // SPAN
SPANS = COLS // SPAN
HALF = SPAN // 2
PIECE = SPAN // NZ
STEPS = NY - 1
DISTANCES = (4, 3, -3, 2, -2, 1, -1, 0)
SLOT = {d: i for i, d in enumerate(DISTANCES)}
HIGHEST = lax.Precision.HIGHEST


def dct_tables():
    k = np.arange(SPAN, dtype=np.float64)[:, None]
    n = np.arange(SPAN, dtype=np.float64)[None, :]
    basis = np.cos(np.pi * (2.0 * n + 1.0) * k / (2.0 * SPAN)) * np.sqrt(2.0 / SPAN)
    basis[0] *= np.sqrt(0.5)
    pair = np.kron(np.eye(2), basis)
    spread = (np.arange(COLS)[None, :] // SPAN == np.arange(SPANS)[:, None]).astype(np.float32)
    return (
        basis.astype(np.float32),
        np.ascontiguousarray(basis.T).astype(np.float32),
        pair.astype(np.float32),
        np.ascontiguousarray(pair.T).astype(np.float32),
        spread,
    )


def step_distance(direction, step):
    distance = 4 - (step + 1) // 2
    half = (step + direction) % 2
    return (distance if direction == 0 else -distance), half


def kernel(
    grad, momentum, counts, blocks, c_in, ct_in, pair_in, pairt_in, spread_in,
    update, residual,
    g_v, m_v, cnt_v, blk_v, c_v, ct_v, pair_v, pairt_v, spread_v,
    stage, other, first, ring, mask, res, inv, zbuf, xbuf, upd,
    load_sem, out_sem, pair_send, pair_recv, ring_send, ring_recv,
    z_send, z_recv, x_send, x_recv, a_send, a_recv,
):
    rep, fsdp = lax.axis_index("rep"), lax.axis_index("fsdp")
    z, x = rep // NX, rep % NX
    y, core = fsdp // NCORE, fsdp % NCORE
    peer = {"fsdp": y * NCORE + 1 - core}
    neighbours = (
        {"fsdp": lax.rem(y + 1, NY) * NCORE + core},
        {"fsdp": lax.rem(y + NY - 1, NY) * NCORE + core},
    )

    def at_z(d):
        return {"rep": lax.rem(z + d, NZ) * NX + x}

    def at_x(d):
        return {"rep": z * NX + lax.rem(x + d, NX)}

    partners = (
        [peer, *neighbours]
        + [at_z(d) for d in range(1, NZ)]
        + [at_x(d) for d in range(1, NX)]
    )

    small = [
        (momentum.at[0], m_v), (counts.at[0], cnt_v), (blocks.at[0], blk_v),
        (c_in, c_v), (ct_in, ct_v), (pair_in, pair_v), (pairt_in, pairt_v), (spread_in, spread_v),
    ]
    loads = [
        pltpu.make_async_copy(
            grad.at[0, 0, pl.ds(k * SPAN, SPAN), :],
            g_v.at[pl.ds(k * SPAN, SPAN), :],
            load_sem.at[k],
        )
        for k in range(CHUNKS)
    ] + [
        pltpu.make_async_copy(src, dst, load_sem.at[CHUNKS + i])
        for i, (src, dst) in enumerate(small)
    ]
    for load in loads:
        load.start()

    barrier = pltpu.get_barrier_semaphore()
    for partner in partners:
        pl.semaphore_signal(barrier, inc=1, device_id=partner, device_id_type=MESH)

    def columns(distance, which):
        target = lax.rem(y + distance + NY, NY) * NCORE + which
        return pl.ds(pl.multiple_of(target * COLS, 128), COLS)

    def pair_copy(k, i):
        return pltpu.make_async_remote_copy(
            src_ref=stage.at[k, i],
            dst_ref=other.at[k, i],
            send_sem=pair_send.at[k, i],
            recv_sem=pair_recv.at[k, i],
            device_id=peer,
            device_id_type=MESH,
        )

    def fill_stage(k, i):
        stage[k, i] = g_v[pl.ds(k * SPAN, SPAN), columns(DISTANCES[i], 1 - core)].astype(F32)

    def own(k, distance, half):
        rows = pl.ds(k * SPAN + half * HALF, HALF)
        return (
            g_v[rows, columns(distance, core)].astype(F32)
            + other[k, SLOT[distance], pl.ds(half * HALF, HALF), :]
        )

    def ring_source(direction, k, step):
        return first.at[direction, k, step] if step < 2 else ring.at[direction, k, step - 2]

    def ring_copy(direction, k, step):
        return pltpu.make_async_remote_copy(
            src_ref=ring_source(direction, k, step),
            dst_ref=ring.at[direction, k, step],
            send_sem=ring_send.at[direction, k, step],
            recv_sem=ring_recv.at[direction, k, step],
            device_id=neighbours[direction],
            device_id_type=MESH,
        )

    def ring_step(k, step):
        needed = {0: (4,), 1: (3, -3), 3: (2, -2), 5: (1, -1)}.get(step, ())
        for distance in needed:
            pair_copy(k, SLOT[distance]).wait_recv()
        for direction in (0, 1):
            distance, half = step_distance(direction, step)
            if distance == -4:
                distance = 4
            if step < 2:
                first[direction, k, step] = own(k, distance, half)
            else:
                ring_copy(direction, k, step - 2).wait_recv()
                ring[direction, k, step - 2] += own(k, distance, half)
            ring_copy(direction, k, step).start()

    def make_mask(k):
        spread = spread_v[...]
        numbers = lax.dot_general(
            blk_v[k].astype(F32), spread, (((0,), (0,)), ((), ())),
            precision=HIGHEST, preferred_element_type=F32,
        )
        live = jnp.dot(
            cnt_v[...].astype(F32), spread, precision=HIGHEST, preferred_element_type=F32
        )[k : k + 1, :]
        slot = lax.broadcasted_iota(jnp.int32, (KMAX, COLS), 0).astype(F32)
        column = lax.broadcasted_iota(jnp.int32, (KMAX, COLS), 1)
        place = numbers - ((column % SPAN) // GRID).astype(F32)
        place = jnp.where(slot + 0.5 < live, place, -100.0)
        for u in range(GRID):
            hit = jnp.where(jnp.abs(place - float(u * GRID)) < 0.5, 1.0, 0.0)
            row = jnp.max(hit, axis=0, keepdims=True)
            mask[pl.ds(k * SPAN + u * GRID, GRID), :] = jnp.broadcast_to(row, (GRID, COLS))

    def right(values, table):
        parts = jnp.concatenate([values[:, g * 128 : (g + 1) * 128] for g in range(3)], axis=0)
        done = jnp.dot(parts, table, precision=HIGHEST, preferred_element_type=F32)
        return jnp.concatenate([done[g * SPAN : (g + 1) * SPAN] for g in range(3)], axis=1)

    def z_copy(k, d):
        return pltpu.make_async_remote_copy(
            src_ref=inv.at[k, lax.rem(z + d, NZ)],
            dst_ref=zbuf.at[k, d - 1],
            send_sem=z_send.at[k, d - 1],
            recv_sem=z_recv.at[k, d - 1],
            device_id=at_z(d),
            device_id_type=MESH,
        )

    def x_copy(k, d):
        return pltpu.make_async_remote_copy(
            src_ref=xbuf.at[k, x],
            dst_ref=xbuf.at[k, x],
            send_sem=x_send.at[k, d - 1],
            recv_sem=x_recv.at[k, d - 1],
            device_id=at_x(d),
            device_id_type=MESH,
        )

    def a_copy(k, d):
        return pltpu.make_async_remote_copy(
            src_ref=upd.at[k, z],
            dst_ref=upd.at[k, z],
            send_sem=a_send.at[k, d - 1],
            recv_sem=a_recv.at[k, d - 1],
            device_id=at_z(d),
            device_id_type=MESH,
        )

    def residual_copy(k):
        rows = pl.ds(k * SPAN, SPAN)
        return pltpu.make_async_copy(res.at[rows, :], residual.at[0, rows, :], out_sem.at[0, k])

    def update_copy(k):
        return pltpu.make_async_copy(upd.at[k], update.at[k], out_sem.at[1, k])

    def finish(k):
        pair_copy(k, SLOT[0]).wait_recv()
        for step in (STEPS - 2, STEPS - 1):
            for direction in (0, 1):
                ring_copy(direction, k, step).wait_recv()
        rows = pl.ds(k * SPAN, SPAN)
        lower = own(k, 0, 0) + ring[0, k, STEPS - 1] + ring[1, k, STEPS - 2]
        upper = own(k, 0, 1) + ring[0, k, STEPS - 2] + ring[1, k, STEPS - 1]
        fresh = 0.9 * m_v[rows, :] + jnp.concatenate([lower, upper], axis=0)
        coeff = right(
            jnp.dot(c_v[...], fresh, precision=HIGHEST, preferred_element_type=F32), pairt_v[...]
        )
        kept = coeff * mask[rows, :]
        decoded = right(
            jnp.dot(ct_v[...], kept, precision=HIGHEST, preferred_element_type=F32), pair_v[...]
        )
        inv[k] = decoded.reshape(NZ, PIECE, COLS)
        for d in range(1, NZ):
            z_copy(k, d).start()
        res[rows, :] = fresh - decoded
        residual_copy(k).start()

    def over_x(k):
        for d in range(1, NZ):
            z_copy(k, d).wait_recv()
        xbuf[k, x] = inv[k, z] + jnp.sum(zbuf[k], axis=0)
        for d in range(1, NX):
            x_copy(k, d).start()

    def gather(k):
        for d in range(1, NX):
            x_copy(k, d).wait_recv()
        upd[k, z] = ((xbuf[k, 0] + xbuf[k, 1]) + (xbuf[k, 2] + xbuf[k, 3])) * (1.0 / (NZ * NX))
        for d in range(1, NZ):
            a_copy(k, d).start()

    def put(k):
        for d in range(1, NZ):
            a_copy(k, d).wait_recv()
        update_copy(k).start()

    loads[0].wait()
    for i in range(NY):
        fill_stage(0, i)
    pl.semaphore_wait(barrier, len(partners))
    for i in range(NY):
        pair_copy(0, i).start()
    for load in loads[1:]:
        load.wait()

    for k in range(CHUNKS + 2):
        here, before, ending, older = k < CHUNKS, 0 < k <= CHUNKS, 1 < k, 2 < k
        for offset in range(7):
            if here and offset % 2 == 0:
                ring_step(k, offset // 2)
            if before and offset % 2 == 1:
                ring_step(k - 1, (offset + 7) // 2)
            if k + 1 < CHUNKS:
                for i in (offset,) if offset < 6 else (6, 7):
                    fill_stage(k + 1, i)
                    pair_copy(k + 1, i).start()
            if here and offset == 1:
                make_mask(k)
            last = k == CHUNKS
            if last and offset == 6:
                finish(k - 1)
            if 1 < k <= CHUNKS:
                if offset == 0:
                    finish(k - 2)
                if offset == 3:
                    over_x(k - 2)
                if offset == 5:
                    gather(k - 2)
            if 2 < k <= CHUNKS + 1 and offset == 1:
                put(k - 3)
    k = CHUNKS - 1
    over_x(k)
    gather(k)
    put(k)

    for k in range(CHUNKS):
        residual_copy(k).wait()
        update_copy(k).wait()
        for i in range(NY):
            pair_copy(k, i).wait_send()
        for direction in (0, 1):
            for step in range(STEPS):
                ring_copy(direction, k, step).wait_send()
        for d in range(1, NZ):
            z_copy(k, d).wait_send()
            a_copy(k, d).wait_send()
        for d in range(1, NX):
            x_copy(k, d).wait_send()


def shards(grad_parts, momentum, keep_counts, keep_blocks):
    tables = [jnp.asarray(t) for t in dct_tables()]
    anywhere = pl.BlockSpec(memory_space=pl.ANY)
    dma = pltpu.SemaphoreType.DMA
    update, residual = pl.pallas_call(
        kernel,
        out_shape=(
            jax.ShapeDtypeStruct((CHUNKS, NZ, PIECE, COLS), F32),
            jax.ShapeDtypeStruct((1, ROWS, COLS), F32),
        ),
        in_specs=[anywhere] * 9,
        out_specs=(anywhere, anywhere),
        scratch_shapes=[
            pltpu.VMEM((ROWS, WIDE), BF16),
            pltpu.VMEM((ROWS, COLS), F32),
            pltpu.VMEM((CHUNKS, SPANS), jnp.int32),
            pltpu.VMEM((CHUNKS, SPANS, KMAX), jnp.int32),
            pltpu.VMEM((SPAN, SPAN), F32),
            pltpu.VMEM((SPAN, SPAN), F32),
            pltpu.VMEM((2 * SPAN, 2 * SPAN), F32),
            pltpu.VMEM((2 * SPAN, 2 * SPAN), F32),
            pltpu.VMEM((SPANS, COLS), F32),
            pltpu.VMEM((CHUNKS, NY, SPAN, COLS), F32),
            pltpu.VMEM((CHUNKS, NY, SPAN, COLS), F32),
            pltpu.VMEM((2, CHUNKS, 2, HALF, COLS), F32),
            pltpu.VMEM((2, CHUNKS, STEPS, HALF, COLS), F32),
            pltpu.VMEM((ROWS, COLS), F32),
            pltpu.VMEM((ROWS, COLS), F32),
            pltpu.VMEM((CHUNKS, NZ, PIECE, COLS), F32),
            pltpu.VMEM((CHUNKS, NZ - 1, PIECE, COLS), F32),
            pltpu.VMEM((CHUNKS, NX, PIECE, COLS), F32),
            pltpu.VMEM((CHUNKS, NZ, PIECE, COLS), F32),
            dma((CHUNKS + 8,)),
            dma((2, CHUNKS)),
            dma((CHUNKS, NY)),
            dma((CHUNKS, NY)),
            dma((2, CHUNKS, STEPS)),
            dma((2, CHUNKS, STEPS)),
            dma((CHUNKS, NZ - 1)),
            dma((CHUNKS, NZ - 1)),
            dma((CHUNKS, NX - 1)),
            dma((CHUNKS, NX - 1)),
            dma((CHUNKS, NZ - 1)),
            dma((CHUNKS, NZ - 1)),
        ],
        compiler_params=pltpu.CompilerParams(
            collective_id=0, has_side_effects=True, vmem_limit_bytes=40 * 1024 * 1024
        ),
        cost_estimate=pl.CostEstimate(
            flops=10**9, bytes_accessed=5 * 10**6, transcendentals=0
        ),
    )(grad_parts, momentum, keep_counts, keep_blocks, *tables)
    return update.reshape(ROWS, COLS), residual


def solution(mesh):
    return jax.shard_map(
        shards,
        mesh=mesh,
        in_specs=(
            P("rep", "fsdp", None, None),
            P("rep", None, "fsdp"),
            P("rep", None, "fsdp"),
            P("rep", None, "fsdp", None),
        ),
        out_specs=(P(None, "fsdp"), P("rep", None, "fsdp")),
        check_vma=False,
    )
```

time: 237 us -> 91.9 us (0.39)
  the two profiles are of different devices: /device:TPU:1 before, /device:TPU:2 now
where the time goes in v1:
time: 91.9 us; the launch traced here: 91.3 us
  Pallas kernels  81 us (88%)
  local copies, waits for them, and re-layouts  9.67 us (11%)
    pallas_call x1, Pallas kernels, shards(): pl.pallas_call(kernel, out_shape=(jax.ShapeDtypeStruct((CHUNKS, NZ, PIECE...  81 us
    unnamed x19, local copies, waits for them, and re-layouts  9.67 us

profile of v1, /device:TPU:2, one launch (start us, length us, event | category | flops | bytes accessed | tf_op | source)
XLA Modules:
  0.0 91.3 jit_solution(5677271081036616247)
XLA Ops:
  0.6 0.7 copy.11.blocks
  1.3 0.0 copy-start
  1.3 1.9 %copy-done = bf16[1,1,256,6144]{3,2,1,0:T(8,128)(2,1)S(1)} copy-done((bf16[1,1,256,6144]{3,2,1,0:T(8,128)(2,1)S(1)}, bf16[1,1,256,6144]{3,2,1,0:T(8,128)(2,1)}, u32[]{:S(2)}) %copy-start) | copy-done | bytes 3145752
  3.2 0.0 copy-start.1
  3.2 1.0 %copy-done.1 = f32[1,256,384]{2,1,0:T(8,128)S(1)} copy-done((f32[1,256,384]{2,1,0:T(8,128)S(1)}, f32[1,256,384]{2,1,0:T(8,128)}, u32[]{:S(2)}) %copy-start.1) | copy-done | bytes 393240
  4.2 0.0 copy-start.2
  4.2 0.8 copy-done.2
  5.1 0.0 copy-start.3
  5.1 0.8 copy-done.3
  5.9 0.0 copy-start.4
  5.9 0.8 copy-done.4
  6.7 0.0 copy-start.5
  6.7 0.8 copy-done.5
  7.4 0.0 copy-start.6
  7.4 0.7 copy-done.6
  8.1 0.0 copy-start.7
  8.1 0.7 copy-done.7
  8.8 81.0 %shard_map.104 = (f32[4,8,8,384]{3,2,1,0:T(8,128)S(1)}, f32[1,256,384]{2,1,0:T(8,128)S(1)}) custom-call(bf16[1,1,256,6144]{3,2,1,0:T(8,128)(2,1)S(1)} %copy-done, f32[1,256,384]{2,1,0:T(8,128)S(1)} %copy-done.1, s32[1,4,6]{2,1,0:T(4,128)S(1)} %copy-done.7, s32[1,4,6,16]{3,2,1,0:T(8,128)S(1)} %copy.11.blocks, f32[64,64]{1,0:T(8,128)S(1)} %copy-done.5, ...), custom_call_target="tpu_custom_call" | custom-call | flops 1000000000 | bytes 5000000 | tf_op jit(solution)/shard_map/pallas_call | solution.py:314
  89.8 0.7 copy.14
  90.6 0.7 copy.15
Async XLA Ops:
  1.3 1.9 %copy-start = (bf16[1,1,256,6144]{3,2,1,0:T(8,128)(2,1)S(1)}, bf16[1,1,256,6144]{3,2,1,0:T(8,128)(2,1)}, u32[]{:S(2)}) copy-start(bf16[1,1,256,6144]{3,2,1,0:T(8,128)(2,1)} %grad.1) | copy-start | bytes 9437188
  3.2 1.0 %copy-start.1 = (f32[1,256,384]{2,1,0:T(8,128)S(1)}, f32[1,256,384]{2,1,0:T(8,128)}, u32[]{:S(2)}) copy-start(f32[1,256,384]{2,1,0:T(8,128)} %momentum.1) | copy-start | bytes 1179652
  4.2 0.8 copy-start.2
  5.1 0.8 copy-start.3
  5.9 0.8 copy-start.4
  6.7 0.8 copy-start.5
  7.4 0.7 copy-start.6
  8.1 0.7 copy-start.7

commit v2 on v1

v2 whole, which is shorter than its diff:
```python
import functools

import jax
import jax.numpy as jnp
import numpy as np
from jax import lax
from jax.experimental import pallas as pl
from jax.experimental.pallas import tpu as pltpu
from jax.sharding import PartitionSpec as P

MESH = pl.DeviceIdType.MESH
F32 = jnp.float32
BF16 = jnp.bfloat16

SPAN = 64
GRID = 8
KMAX = 16
NZ, NX, NY, NCORE = 8, 4, 8, 2
ROWS, COLS, WIDE = 256, 384, 6144
CHUNKS = ROWS // SPAN
SPANS = COLS // SPAN
HALF = SPAN // 2
PIECE = SPAN // NZ
STEPS = NY - 1
VMEM_LIMIT = 62 * 2**20
DISTANCES = (4, 3, -3, 2, -2, 1, -1, 0)
SLOT = {d: i for i, d in enumerate(DISTANCES)}
HIGHEST = lax.Precision.HIGHEST
VMEM_LIMIT = 62 * 2**20
UNITS = ((0, 0, 3), (1, 0, 3), (2, 0, 3), (3, 0, 2), (3, 2, 3))
ORDER = [
    (int(name[0]), int(name[1]))
    for name in (
        "00 10 01 20 02 11 12 03 04 13 14 05 06 15 16 "
        "30 40 21 22 31 32 41 42 23 24 33 34 43 44 25 26 35 36 45 46"
    ).split()
]
FINISH, OVER_X, GATHER, MASK, EXCHANGE = "finish", "over_x", "gather", "mask", "exchange"
TASKS = {
    0: [(EXCHANGE, 2)],
    2: [(EXCHANGE, 3)],
    5: [(MASK, 0)],
    7: [(MASK, 1)],
    9: [(MASK, 2)],
    11: [(MASK, 3)],
    17: [(FINISH, 0)],
    19: [(FINISH, 1)],
    24: [(OVER_X, 0)],
    26: [(OVER_X, 1)],
    28: [(GATHER, 0)],
    30: [(GATHER, 1)],
}
TAIL = [(task, unit) for task in (FINISH, OVER_X, GATHER) for unit in (2, 3, 4)]


def dct_tables():
    k = np.arange(SPAN, dtype=np.float64)[:, None]
    n = np.arange(SPAN, dtype=np.float64)[None, :]
    basis = np.cos(np.pi * (2.0 * n + 1.0) * k / (2.0 * SPAN)) * np.sqrt(2.0 / SPAN)
    basis[0] *= np.sqrt(0.5)
    pair = np.kron(np.eye(2), basis)
    return np.stack([pair.T, pair]).astype(np.float32)


def split_table(table, axis):
    high = table.astype(BF16)
    low = (table - high.astype(F32)).astype(BF16)
    return jnp.concatenate([high, high, low], axis=axis)


def split(values, axis):
    high = values.astype(BF16)
    low = (values - high.astype(F32)).astype(BF16)
    return jnp.concatenate([high, low, high], axis=axis)


def step_distance(direction, step):
    distance = 4 - (step + 1) // 2
    half = (step + direction) % 2
    return (distance if direction == 0 else -distance), half


def kernel(
    grad, momentum, counts, blocks, tables,
    update, residual,
    g_v, m_v, cnt_v, blk_v, tab_v, left_v, right_v,
    stage, other, first, ring, mask, res, inv, zbuf, xbuf, upd,
    load_sem, res_sem, upd_sem, pair_send, pair_recv, ring_send, ring_recv,
    z_send, z_recv, x_send, x_recv, a_send, a_recv,
):
    rep, fsdp = lax.axis_index("rep"), lax.axis_index("fsdp")
    z, x = rep // NX, rep % NX
    y, core = fsdp // NCORE, fsdp % NCORE
    peer = {"fsdp": y * NCORE + 1 - core}
    neighbours = (
        {"fsdp": lax.rem(y + 1, NY) * NCORE + core},
        {"fsdp": lax.rem(y + NY - 1, NY) * NCORE + core},
    )

    def at_z(d):
        return {"rep": lax.rem(z + d, NZ) * NX + x}

    def at_x(d):
        return {"rep": z * NX + lax.rem(x + d, NX)}

    partners = (
        [peer, *neighbours]
        + [at_z(d) for d in range(1, NZ)]
        + [at_x(d) for d in range(1, NX)]
    )

    small = [
        (counts.at[0], cnt_v), (blocks.at[0], blk_v),
        (tables, tab_v), (momentum.at[0], m_v),
    ]
    loads = [
        pltpu.make_async_copy(
            grad.at[0, 0, pl.ds(k * SPAN, SPAN), :],
            g_v.at[pl.ds(k * SPAN, SPAN), :],
            load_sem.at[k],
        )
        for k in range(CHUNKS)
    ] + [
        pltpu.make_async_copy(src, dst, load_sem.at[CHUNKS + i])
        for i, (src, dst) in enumerate(small)
    ]
    for load in loads:
        load.start()

    barrier = pltpu.get_barrier_semaphore()
    for partner in partners:
        pl.semaphore_signal(barrier, inc=1, device_id=partner, device_id_type=MESH)

    def columns(distance, which, first_lane=0, width=COLS):
        target = lax.rem(y + distance + NY, NY) * NCORE + which
        return pl.ds(pl.multiple_of(target * COLS + first_lane, 128), width)

    def lanes(unit):
        _, low, high = UNITS[unit]
        return pl.ds(low * 128, (high - low) * 128)

    def moved(src, dst, send_sem, recv_sem, device):
        return pltpu.make_async_remote_copy(
            src_ref=src, dst_ref=dst, send_sem=send_sem, recv_sem=recv_sem,
            device_id=device, device_id_type=MESH,
        )

    def pair_copy(k, i):
        return moved(stage.at[k, i], other.at[k, i], pair_send, pair_recv.at[k, i], peer)

    def fill_stage(k, i):
        stage[k, i] = g_v[pl.ds(k * SPAN, SPAN), columns(DISTANCES[i], 1 - core)].astype(F32)

    exchanged = set()

    def need(k, distance):
        if (k, distance) not in exchanged:
            exchanged.add((k, distance))
            pair_copy(k, SLOT[distance]).wait_recv()

    def own(unit, distance, half):
        k, low, high = UNITS[unit]
        need(k, distance)
        return (
            g_v[
                pl.ds(k * SPAN + half * HALF, HALF),
                columns(distance, core, low * 128, (high - low) * 128),
            ].astype(F32)
            + other[k, SLOT[distance], pl.ds(half * HALF, HALF), lanes(unit)]
        )

    def ring_copy(direction, unit, step):
        k, window = UNITS[unit][0], lanes(unit)
        return moved(
            first.at[direction, k, step, :, window]
            if step < 2
            else ring.at[direction, k, step - 2, :, window],
            ring.at[direction, k, step, :, window],
            ring_send.at[direction],
            ring_recv.at[direction, unit, step],
            neighbours[direction],
        )

    def ring_step(unit, step):
        k, window = UNITS[unit][0], lanes(unit)
        for direction in (0, 1):
            distance, half = step_distance(direction, step)
            if distance == -4:
                distance = 4
            if step < 2:
                first[direction, k, step, :, window] = own(unit, distance, half)
            else:
                ring_copy(direction, unit, step - 2).wait_recv()
                ring[direction, k, step - 2, :, window] += own(unit, distance, half)
            ring_copy(direction, unit, step).start()

    def make_mask(k):
        spread = jnp.where(
            lax.broadcasted_iota(jnp.int32, (SPANS, COLS), 1) // SPAN
            == lax.broadcasted_iota(jnp.int32, (SPANS, COLS), 0),
            1.0, 0.0,
        )
        numbers = lax.dot_general(
            blk_v[:, k, :].astype(F32), spread, (((0,), (0,)), ((), ())),
            precision=HIGHEST, preferred_element_type=F32,
        )
        live = jnp.dot(
            cnt_v[...].astype(F32), spread, precision=HIGHEST, preferred_element_type=F32
        )[k : k + 1, :]
        slot = lax.broadcasted_iota(jnp.int32, (KMAX, COLS), 0).astype(F32)
        column = lax.broadcasted_iota(jnp.int32, (KMAX, COLS), 1)
        place = numbers - ((column % SPAN) // GRID).astype(F32)
        place = jnp.where(slot + 0.5 < live, place, -100.0)
        for u in range(GRID):
            hit = jnp.where(jnp.abs(place - float(u * GRID)) < 0.5, 1.0, 0.0)
            row = jnp.max(hit, axis=0, keepdims=True)
            mask[pl.ds(k * SPAN + u * GRID, GRID), :] = jnp.broadcast_to(row, (GRID, COLS))

    def transform(values, way):
        groups = values.shape[1] // 128
        rows = jnp.dot(left_v[way], split(values, 0), preferred_element_type=F32)
        parts = jnp.concatenate([rows[:, g * 128 : (g + 1) * 128] for g in range(groups)], axis=0)
        done = jnp.dot(split(parts, 1), right_v[way], preferred_element_type=F32)
        return jnp.concatenate([done[g * SPAN : (g + 1) * SPAN] for g in range(groups)], axis=1)

    def z_copy(unit, d):
        k, window = UNITS[unit][0], lanes(unit)
        return moved(
            inv.at[k, lax.rem(z + d, NZ), :, window], zbuf.at[k, d - 1, :, window],
            z_send, z_recv.at[unit], at_z(d),
        )

    def x_copy(unit, d):
        k, window = UNITS[unit][0], lanes(unit)
        return moved(
            xbuf.at[k, x, :, window], xbuf.at[k, x, :, window],
            x_send, x_recv.at[unit], at_x(d),
        )

    def a_copy(unit, d):
        k, window = UNITS[unit][0], lanes(unit)
        return moved(
            upd.at[k, :, window], update.at[k, z, :, window],
            a_send, a_recv.at[unit], at_z(d),
        )

    def arrived(ref, sem):
        moved(ref, ref, z_send, sem, peer).wait_recv()

    def sent(ref, sem):
        moved(ref, ref, sem, z_recv.at[0], peer).wait_send()

    def residual_copy(unit):
        rows, window = pl.ds(UNITS[unit][0] * SPAN, SPAN), lanes(unit)
        return pltpu.make_async_copy(res.at[rows, window], residual.at[0, rows, window], res_sem)

    def update_copy(unit):
        k, window = UNITS[unit][0], lanes(unit)
        return pltpu.make_async_copy(upd.at[k, :, window], update.at[k, z, :, window], upd_sem)

    def finish(unit):
        k, window = UNITS[unit][0], lanes(unit)
        need(k, 0)
        for step in (STEPS - 2, STEPS - 1):
            for direction in (0, 1):
                ring_copy(direction, unit, step).wait_recv()
        rows = pl.ds(k * SPAN, SPAN)
        lower = (
            own(unit, 0, 0) + ring[0, k, STEPS - 1, :, window] + ring[1, k, STEPS - 2, :, window]
        )
        upper = (
            own(unit, 0, 1) + ring[0, k, STEPS - 2, :, window] + ring[1, k, STEPS - 1, :, window]
        )
        fresh = 0.9 * m_v[rows, window] + jnp.concatenate([lower, upper], axis=0)
        decoded = transform(transform(fresh, 0) * mask[rows, window], 1)
        inv[k, :, :, window] = decoded.reshape(NZ, PIECE, decoded.shape[1])
        for d in (4, 3, 5, 2, 6, 1, 7):
            z_copy(unit, d).start()
        res[rows, window] = fresh - decoded
        residual_copy(unit).start()

    def over_x(unit):
        k, window = UNITS[unit][0], lanes(unit)
        arrived(zbuf.at[k, :, :, window], z_recv.at[unit])
        xbuf[k, x, :, window] = inv[k, z, :, window] + jnp.sum(zbuf[k, :, :, window], axis=0)
        for d in (2, 1, 3):
            x_copy(unit, d).start()

    def gather(unit):
        k, window = UNITS[unit][0], lanes(unit)
        arrived(xbuf.at[k, pl.ds(0, NX - 1), :, window], x_recv.at[unit])
        total = (xbuf[k, 0, :, window] + xbuf[k, 1, :, window]) + (
            xbuf[k, 2, :, window] + xbuf[k, 3, :, window]
        )
        upd[k, :, window] = total * (1.0 / (NZ * NX))
        for d in (4, 3, 5, 2, 6, 1, 7):
            a_copy(unit, d).start()
        update_copy(unit).start()

    def exchange(k):
        for i in range(NY):
            fill_stage(k, i)
            pair_copy(k, i).start()

    loads[0].wait()
    for i in range(NY):
        fill_stage(0, i)
    pl.semaphore_wait(barrier, len(partners))
    for i in range(NY):
        pair_copy(0, i).start()
    for load in loads[1:]:
        load.wait()
    exchange(1)

    tasks = {FINISH: finish, OVER_X: over_x, GATHER: gather, MASK: make_mask, EXCHANGE: exchange}
    for place, (unit, step) in enumerate(ORDER):
        ring_step(unit, step)
        if place == 3:
            for way in range(2):
                left_v[way] = split_table(tab_v[1 - way, :SPAN, :SPAN], 1)
                right_v[way] = split_table(tab_v[way], 0)
        for task, what in TASKS.get(place, ()):
            tasks[task](what)
    for task, what in TAIL:
        tasks[task](what)

    pltpu.make_async_copy(res, residual.at[0], res_sem).wait()
    pltpu.make_async_copy(upd, update.at[:, z], upd_sem).wait()
    sent(stage, pair_send)
    for direction in (0, 1):
        sent(ring.at[direction], ring_send.at[direction])
    sent(zbuf, z_send)
    sent(xbuf.at[:, pl.ds(0, NX - 1)], x_send)
    for unit in range(len(UNITS)):
        arrived(zbuf.at[UNITS[unit][0], :, :, lanes(unit)], a_recv.at[unit])
    sent(zbuf, a_send)


def shards(grad_parts, momentum, keep_counts, keep_blocks):
    anywhere = pl.BlockSpec(memory_space=pl.ANY)
    outside = pl.BlockSpec(memory_space=pltpu.HBM)
    dma = pltpu.SemaphoreType.DMA
    update, residual = pl.pallas_call(
        kernel,
        out_shape=(
            pltpu.VMEM((CHUNKS, NZ, PIECE, COLS), F32),
            pltpu.VMEM((1, ROWS, COLS), F32),
        ),
        in_specs=[outside] * 5,
        out_specs=(anywhere, anywhere),
        scratch_shapes=[
            pltpu.VMEM((ROWS, WIDE), BF16),
            pltpu.VMEM((ROWS, COLS), F32),
            pltpu.VMEM((CHUNKS, SPANS), jnp.int32),
            pltpu.VMEM((SPANS, CHUNKS, KMAX), jnp.int32),
            pltpu.VMEM((2, 2 * SPAN, 2 * SPAN), F32),
            pltpu.VMEM((2, SPAN, 3 * SPAN), BF16),
            pltpu.VMEM((2, 6 * SPAN, 2 * SPAN), BF16),
            pltpu.VMEM((CHUNKS, NY, SPAN, COLS), F32),
            pltpu.VMEM((CHUNKS, NY, SPAN, COLS), F32),
            pltpu.VMEM((2, CHUNKS, 2, HALF, COLS), F32),
            pltpu.VMEM((2, CHUNKS, STEPS, HALF, COLS), F32),
            pltpu.VMEM((ROWS, COLS), F32),
            pltpu.VMEM((ROWS, COLS), F32),
            pltpu.VMEM((CHUNKS, NZ, PIECE, COLS), F32),
            pltpu.VMEM((CHUNKS, NZ - 1, PIECE, COLS), F32),
            pltpu.VMEM((CHUNKS, NX, PIECE, COLS), F32),
            pltpu.VMEM((CHUNKS, PIECE, COLS), F32),
            dma((CHUNKS + 4,)),
            dma,
            dma,
            dma,
            dma((CHUNKS, NY)),
            dma((2,)),
            dma((2, len(UNITS), STEPS)),
            dma,
            dma((len(UNITS),)),
            dma,
            dma((len(UNITS),)),
            dma,
            dma((len(UNITS),)),
        ],
        compiler_params=pltpu.CompilerParams(
            collective_id=0, has_side_effects=True, vmem_limit_bytes=VMEM_LIMIT
        ),
        cost_estimate=pl.CostEstimate(
            flops=10**9, bytes_accessed=5 * 10**6, transcendentals=0
        ),
    )(grad_parts, momentum, keep_counts, keep_blocks.transpose(0, 2, 1, 3), jnp.asarray(dct_tables()))
    return update.reshape(ROWS, COLS), residual


def solution(mesh):
    return jax.shard_map(
        shards,
        mesh=mesh,
        in_specs=(
            P("rep", "fsdp", None, None),
            P("rep", None, "fsdp"),
            P("rep", None, "fsdp"),
            P("rep", None, "fsdp", None),
        ),
        out_specs=(P(None, "fsdp"), P("rep", None, "fsdp")),
        check_vma=False,
    )
```

time: 91.9 us -> 64.1 us (0.70)
  the two profiles are of different devices: /device:TPU:2 before, /device:TPU:24 now
where the time goes in v2:
time: 64.1 us; the launch traced here: 63.9 us
  Pallas kernels  61.8 us (96%)
  local copies, waits for them, and re-layouts  1.49 us (2%)
    pallas_call x1, Pallas kernels, shards(): pl.pallas_call(kernel, out_shape=(pltpu.VMEM((CHUNKS, NZ, PIECE, COLS), F...  61.8 us
    unnamed x2, local copies, waits for them, and re-layouts  1.49 us

profile of v2, /device:TPU:24, one launch (start us, length us, event | category | flops | bytes accessed | tf_op | source)
XLA Modules:
  0.0 63.9 jit_solution(259117808991113016)
XLA Ops:
  0.6 61.8 %shard_map.68 = (f32[4,8,8,384]{3,2,1,0:T(8,128)S(1)}, f32[1,256,384]{2,1,0:T(8,128)S(1)}) custom-call(bf16[1,1,256,6144]{3,2,1,0:T(8,128)(2,1)} %grad.1, f32[1,256,384]{2,1,0:T(8,128)} %momentum.1, s32[1,4,6]{2,1,0:T(4,128)} %counts.1, s32[1,6,4,16]{3,2,1,0:T(4,128)} %bitcast.3, f32[2,128,128]{2,1,0:T(8,128)} %constant.2.clone.tables), custom_call_target="tpu_custom_call" | custom-call | flops 1000000000 | bytes 5000000 | tf_op jit(solution)/shard_map/pallas_call | solution.py:343
  62.5 0.7 %copy.9 = f32[256,384]{1,0:T(8,128)} copy(f32[256,384]{1,0:T(8,128)S(1)} %bitcast.2) | data formatting | bytes 786432
  63.2 0.7 %copy.10 = f32[1,256,384]{2,1,0:T(8,128)} copy(f32[1,256,384]{2,1,0:T(8,128)S(1)} %get-tuple-element.7) | data formatting | bytes 786432

commit v3 on v2

--- a/solution.py
+++ b/solution.py
@@ -27,30 +27,29 @@
 SLOT = {d: i for i, d in enumerate(DISTANCES)}
 HIGHEST = lax.Precision.HIGHEST
 VMEM_LIMIT = 62 * 2**20
-UNITS = ((0, 0, 3), (1, 0, 3), (2, 0, 3), (3, 0, 2), (3, 2, 3))
-ORDER = [
-    (int(name[0]), int(name[1]))
-    for name in (
-        "00 10 01 20 02 11 12 03 04 13 14 05 06 15 16 "
-        "30 40 21 22 31 32 41 42 23 24 33 34 43 44 25 26 35 36 45 46"
-    ).split()
-]
-FINISH, OVER_X, GATHER, MASK, EXCHANGE = "finish", "over_x", "gather", "mask", "exchange"
-TASKS = {
-    0: [(EXCHANGE, 2)],
-    2: [(EXCHANGE, 3)],
-    5: [(MASK, 0)],
-    7: [(MASK, 1)],
-    9: [(MASK, 2)],
-    11: [(MASK, 3)],
-    17: [(FINISH, 0)],
-    19: [(FINISH, 1)],
-    24: [(OVER_X, 0)],
-    26: [(OVER_X, 1)],
-    28: [(GATHER, 0)],
-    30: [(GATHER, 1)],
-}
-TAIL = [(task, unit) for task in (FINISH, OVER_X, GATHER) for unit in (2, 3, 4)]
+UNITS = ((0, 0, 3), (1, 0, 3), (2, 0, 3), (3, 0, 3))
+GROUPS = ((2, 0), (2, 1), (2, 2), (3, 0), (3, 1), (3, 2))
+NG = len(GROUPS)
+SKIP = 2 * GROUPS[0][1]
+WIDTH = NG * 128
+LISTED = 2 * NG * GRID
+HALF_LISTED = LISTED // 2
+ROW0 = GROUPS[0][0]
+EARLY = tuple(u for u in range(len(UNITS)) if UNITS[u][0] < ROW0)
+LATE = tuple(u for u in range(len(UNITS)) if UNITS[u][0] >= ROW0)
+EXCHANGE, RING, SPREAD, PLACE, PICK, LIST, MASK, FINISH, OVER_X, GATHER, DECODE, LAST = range(12)
+PROGRAM = (
+    [(RING, 0, 0), (EXCHANGE, 0, 4, 8), (RING, 0, 1), (EXCHANGE, 1, 0, 8), (RING, 1, 0), (RING, 1, 1)]
+    + [(EXCHANGE, 3, 0, 8), (EXCHANGE, 2, 0, 8), (SPREAD,), (RING, 0, 2), (PICK, 4), (RING, 0, 3)]
+    + [(LIST, 0), (PICK, 3), (PICK, -3), (RING, 1, 2), (LIST, 1), (RING, 0, 4), (RING, 0, 5)]
+    + [(LIST, 2), (RING, 1, 3), (PICK, 2), (PICK, -2), (LIST, 3), (RING, 0, 6), (PICK, 1), (LIST, 4)]
+    + [(PICK, -1), (RING, 1, 4), (LIST, 5), (MASK, 0), (RING, 1, 5), (FINISH, 0), (LIST, 6)]
+    + [(RING, 1, 6), (RING, 2, 0), (RING, 3, 0), (RING, 2, 1), (RING, 3, 1), (PICK, 0), (PLACE,)]
+    + [(DECODE,), (MASK, 1), (FINISH, 1), (RING, 2, 2), (RING, 3, 2), (OVER_X, 0), (RING, 2, 3)]
+    + [(RING, 3, 3), (RING, 2, 4), (GATHER, 0), (RING, 3, 4), (OVER_X, 2), (RING, 2, 5)]
+    + [(OVER_X, 3), (RING, 3, 5), (RING, 2, 6), (GATHER, 2), (OVER_X, 1), (RING, 3, 6)]
+    + [(GATHER, 3), (LAST, 2), (GATHER, 1), (LAST, 3)]
+)
 
 
 def dct_tables():
@@ -84,18 +83,19 @@
     grad, momentum, counts, blocks, tables,
     update, residual,
     g_v, m_v, cnt_v, blk_v, tab_v, left_v, right_v,
-    stage, other, first, ring, mask, res, inv, zbuf, xbuf, upd,
+    tile, tiles, spread_v, place_v, packed, brought, stage, other, first, ring, mask, res, inv, zbuf, xbuf, upd,
     load_sem, res_sem, upd_sem, pair_send, pair_recv, ring_send, ring_recv,
-    z_send, z_recv, x_send, x_recv, a_send, a_recv,
+    tile_send, tile_recv, list_send, list_recv, z_send, z_recv, x_send, x_recv, a_send, a_recv,
 ):
     rep, fsdp = lax.axis_index("rep"), lax.axis_index("fsdp")
     z, x = rep // NX, rep % NX
     y, core = fsdp // NCORE, fsdp % NCORE
     peer = {"fsdp": y * NCORE + 1 - core}
-    neighbours = (
-        {"fsdp": lax.rem(y + 1, NY) * NCORE + core},
-        {"fsdp": lax.rem(y + NY - 1, NY) * NCORE + core},
-    )
+
+    def at_y(d):
+        return {"fsdp": lax.rem(y + d, NY) * NCORE + core}
+
+    neighbours = (at_y(1), at_y(NY - 1))
 
     def at_z(d):
         return {"rep": lax.rem(z + d, NZ) * NX + x}
@@ -104,7 +104,8 @@
         return {"rep": z * NX + lax.rem(x + d, NX)}
 
     partners = (
-        [peer, *neighbours]
+        [peer]
+        + [at_y(d) for d in range(1, NY)]
         + [at_z(d) for d in range(1, NZ)]
         + [at_x(d) for d in range(1, NX)]
     )
@@ -194,27 +195,176 @@
                 ring[direction, k, step - 2, :, window] += own(unit, distance, half)
             ring_copy(direction, unit, step).start()
 
-    def make_mask(k):
+    def places(k):
         spread = jnp.where(
             lax.broadcasted_iota(jnp.int32, (SPANS, COLS), 1) // SPAN
             == lax.broadcasted_iota(jnp.int32, (SPANS, COLS), 0),
             1.0, 0.0,
-        )
+        ).astype(BF16)
         numbers = lax.dot_general(
-            blk_v[:, k, :].astype(F32), spread, (((0,), (0,)), ((), ())),
-            precision=HIGHEST, preferred_element_type=F32,
+            blk_v[:, k, :].astype(F32).astype(BF16), spread, (((0,), (0,)), ((), ())),
+            preferred_element_type=F32,
         )
         live = jnp.dot(
-            cnt_v[...].astype(F32), spread, precision=HIGHEST, preferred_element_type=F32
+            cnt_v[...].astype(F32).astype(BF16), spread, preferred_element_type=F32
         )[k : k + 1, :]
         slot = lax.broadcasted_iota(jnp.int32, (KMAX, COLS), 0).astype(F32)
         column = lax.broadcasted_iota(jnp.int32, (KMAX, COLS), 1)
         place = numbers - ((column % SPAN) // GRID).astype(F32)
-        place = jnp.where(slot + 0.5 < live, place, -100.0)
+        return jnp.where(slot + 0.5 < live, place, -100.0)
+
+    def make_mask(k):
+        place = places(k)
         for u in range(GRID):
-            hit = jnp.where(jnp.abs(place - float(u * GRID)) < 0.5, 1.0, 0.0)
+            hit = jnp.where(place == float(u * GRID), 1.0, 0.0)
             row = jnp.max(hit, axis=0, keepdims=True)
             mask[pl.ds(k * SPAN + u * GRID, GRID), :] = jnp.broadcast_to(row, (GRID, COLS))
+
+    def make_tile():
+        span = lax.broadcasted_iota(jnp.int32, (SPANS, 128), 0)
+        lane = lax.broadcasted_iota(jnp.int32, (SPANS, 128), 1)
+        total = jnp.zeros((GRID, 128), F32)
+        for k in range(ROW0, CHUNKS):
+            listed = blk_v[:, k, :].astype(F32).astype(BF16)
+            at = span + (k - ROW0) * SPANS - SKIP
+            for h in range(2):
+                chosen = jnp.where((lane == at + 64 * h) & (at >= 0), 1.0, 0.0).astype(BF16)
+                moved_out = lax.dot_general(
+                    listed, chosen, (((0,), (0,)), ((), ())), preferred_element_type=F32
+                )
+                total = total + moved_out[h * GRID : (h + 1) * GRID]
+        tile[...] = total
+
+    def make_spread():
+        lane = lax.broadcasted_iota(jnp.int32, (128, WIDTH), 0)
+        span = lax.broadcasted_iota(jnp.int32, (128, WIDTH), 1) // SPAN
+        for h in range(2):
+            spread_v[h] = jnp.where(lane == span + 64 * h, 1.0, 0.0).astype(BF16)
+
+    def tile_copy(d):
+        return moved(tile, tiles.at[d - 1], tile_send, tile_recv, at_y(d))
+
+    def listed_place(distance):
+        source = tile[...] if distance == 0 else tiles[7 - distance % NY]
+        column = lax.broadcasted_iota(jnp.int32, (GRID, WIDTH), 1)
+        group = ((column % SPAN) // GRID).astype(F32)
+        return jnp.concatenate(
+            [
+                jnp.dot(source.astype(BF16), spread_v[h], preferred_element_type=F32) - group
+                for h in range(2)
+            ],
+            axis=0,
+        )
+
+    def lane_bit(size):
+        lane = lax.broadcasted_iota(jnp.int32, (LISTED, 128), 1)
+        return (lane // size) % 2 == 1
+
+    def listed_sum(distance):
+        fields = {}
+        for k in range(ROW0, CHUNKS):
+            rows = pl.ds(k * SPAN, SPAN)
+            need(k, distance)
+            field = g_v[rows, columns(distance, core)].astype(F32) + other[k, SLOT[distance]]
+            if distance == 0:
+                field = field + 0.9 * m_v[rows, :]
+            fields[k] = field
+        field = jnp.concatenate([fields[k][:, g * 128 : (g + 1) * 128] for k, g in GROUPS], axis=1)
+        coeff = transform(field, 0)
+        place = listed_place(distance)
+        picked = []
+        for slot in range(KMAX):
+            where = jnp.broadcast_to(place[slot : slot + 1, :], (GRID, WIDTH))
+            got = jnp.zeros((GRID, WIDTH), F32)
+            for u in range(GRID):
+                got = jnp.where(where == float(u * GRID), coeff[u * GRID : (u + 1) * GRID], got)
+            picked.append(got)
+        values = [
+            jnp.concatenate(
+                [
+                    picked[h * GRID + j][:, g * 128 : (g + 1) * 128]
+                    for h in range(2)
+                    for g in range(NG)
+                ],
+                axis=0,
+            )
+            for j in range(GRID)
+        ]
+        for size in (32, 16, 8):
+            bit = lane_bit(size)
+            half = len(values) // 2
+            merged = []
+            for j in range(half):
+                low, high = values[j], values[j + half]
+                out = jnp.where(bit, low, high)
+                out = jnp.where(bit, pltpu.roll(out, size, 1), pltpu.roll(out, 128 - size, 1))
+                merged.append(jnp.where(bit, high, low) + out)
+            values = merged
+        packed[SLOT[distance]] = values[0]
+
+    def half_rows(half):
+        return pl.ds(half * HALF_LISTED, HALF_LISTED)
+
+    def list_copy(direction, step):
+        if step < 2:
+            distance, half = step_distance(direction, step)
+            source = packed.at[SLOT[4 if distance == -4 else distance], half_rows(half)]
+        else:
+            source = brought.at[direction, step - 2]
+        return moved(
+            source, brought.at[direction, step],
+            list_send.at[direction], list_recv.at[direction, step], neighbours[direction],
+        )
+
+    def list_step(step):
+        for direction in (0, 1):
+            distance, half = step_distance(direction, step)
+            if step >= 2:
+                list_copy(direction, step - 2).wait_recv()
+                brought[direction, step - 2] += packed[SLOT[distance], half_rows(half)]
+            list_copy(direction, step).start()
+
+    def decode():
+        for step in (STEPS - 2, STEPS - 1):
+            for direction in (0, 1):
+                list_copy(direction, step).wait_recv()
+        own_part = packed[SLOT[0]]
+        values = [
+            own_part
+            + jnp.concatenate(
+                [
+                    brought[0, STEPS - 1] + brought[1, STEPS - 2],
+                    brought[0, STEPS - 2] + brought[1, STEPS - 1],
+                ],
+                axis=0,
+            )
+        ]
+        for size in (8, 16, 32):
+            bit = lane_bit(size)
+            low, high = [], []
+            for value in values:
+                low.append(jnp.where(bit, pltpu.roll(value, size, 1), value))
+                high.append(jnp.where(bit, value, pltpu.roll(value, 128 - size, 1)))
+            values = low + high
+        place = jnp.concatenate(
+            [place_v[k - ROW0][:, g * 128 : (g + 1) * 128] for k, g in GROUPS], axis=1
+        )
+        kept = [jnp.zeros((GRID, WIDTH), F32)] * GRID
+        for slot in range(KMAX):
+            h, j = slot // GRID, slot % GRID
+            at = [(h * NG + g) * GRID for g in range(NG)]
+            value = jnp.concatenate([values[j][r : r + GRID] for r in at], axis=1)
+            where = jnp.broadcast_to(place[slot : slot + 1, :], (GRID, WIDTH))
+            kept = [
+                jnp.where(where == float(u * GRID), value, kept[u]) for u in range(GRID)
+            ]
+        decoded = transform(jnp.concatenate(kept, axis=0), 1)
+        for i, (k, g) in enumerate(GROUPS):
+            window = pl.ds(g * 128, 128)
+            inv[k, :, :, window] = decoded[:, i * 128 : (i + 1) * 128].reshape(NZ, PIECE, 128)
+        for unit in LATE:
+            for d in (4, 3, 5, 2, 6, 1, 7):
+                z_copy(unit, d).start()
 
     def transform(values, way):
         groups = values.shape[1] // 128
@@ -258,20 +408,24 @@
         k, window = UNITS[unit][0], lanes(unit)
         return pltpu.make_async_copy(upd.at[k, :, window], update.at[k, z, :, window], upd_sem)
 
-    def finish(unit):
-        k, window = UNITS[unit][0], lanes(unit)
-        need(k, 0)
+    def summed(unit):
+        k, window = UNITS[unit][0], lanes(unit)
         for step in (STEPS - 2, STEPS - 1):
             for direction in (0, 1):
                 ring_copy(direction, unit, step).wait_recv()
-        rows = pl.ds(k * SPAN, SPAN)
         lower = (
             own(unit, 0, 0) + ring[0, k, STEPS - 1, :, window] + ring[1, k, STEPS - 2, :, window]
         )
         upper = (
             own(unit, 0, 1) + ring[0, k, STEPS - 2, :, window] + ring[1, k, STEPS - 1, :, window]
         )
-        fresh = 0.9 * m_v[rows, window] + jnp.concatenate([lower, upper], axis=0)
+        rows = pl.ds(k * SPAN, SPAN)
+        return 0.9 * m_v[rows, window] + jnp.concatenate([lower, upper], axis=0)
+
+    def finish(unit):
+        k, window = UNITS[unit][0], lanes(unit)
+        rows = pl.ds(k * SPAN, SPAN)
+        fresh = summed(unit)
         decoded = transform(transform(fresh, 0) * mask[rows, window], 1)
         inv[k, :, :, window] = decoded.reshape(NZ, PIECE, decoded.shape[1])
         for d in (4, 3, 5, 2, 6, 1, 7):
@@ -279,6 +433,12 @@
         res[rows, window] = fresh - decoded
         residual_copy(unit).start()
 
+    def last(unit):
+        k, window = UNITS[unit][0], lanes(unit)
+        rows = pl.ds(k * SPAN, SPAN)
+        res[rows, window] = summed(unit) - inv[k, :, :, window].reshape(SPAN, COLS)
+        residual_copy(unit).start()
+
     def over_x(unit):
         k, window = UNITS[unit][0], lanes(unit)
         arrived(zbuf.at[k, :, :, window], z_recv.at[unit])
@@ -297,38 +457,53 @@
             a_copy(unit, d).start()
         update_copy(unit).start()
 
-    def exchange(k):
+    def exchange(k, begin, end):
+        if k > 1:
+            for i in range(begin, end):
+                fill_stage(k, i)
+        for i in range(begin, end):
+            pair_copy(k, i).start()
+
+    def spread_tables():
+        for way in range(2):
+            left_v[way] = split_table(tab_v[1 - way, :SPAN, :SPAN], 1)
+            right_v[way] = split_table(tab_v[way], 0)
+        make_spread()
+        arrived(tiles, tile_recv)
+
+    def late_places():
+        for k in range(ROW0, CHUNKS):
+            place_v[k - ROW0] = places(k)
+
+    for load in loads[CHUNKS : CHUNKS + 2]:
+        load.wait()
+    make_tile()
+    for k in range(2):
+        loads[k].wait()
         for i in range(NY):
             fill_stage(k, i)
-            pair_copy(k, i).start()
-
-    loads[0].wait()
-    for i in range(NY):
-        fill_stage(0, i)
     pl.semaphore_wait(barrier, len(partners))
-    for i in range(NY):
-        pair_copy(0, i).start()
-    for load in loads[1:]:
+    exchange(0, 0, 4)
+    for d in (4, 3, 5, 2, 6, 1, 7):
+        tile_copy(d).start()
+    for load in loads[2:CHUNKS] + loads[CHUNKS + 2 :]:
         load.wait()
-    exchange(1)
-
-    tasks = {FINISH: finish, OVER_X: over_x, GATHER: gather, MASK: make_mask, EXCHANGE: exchange}
-    for place, (unit, step) in enumerate(ORDER):
-        ring_step(unit, step)
-        if place == 3:
-            for way in range(2):
-                left_v[way] = split_table(tab_v[1 - way, :SPAN, :SPAN], 1)
-                right_v[way] = split_table(tab_v[way], 0)
-        for task, what in TASKS.get(place, ()):
-            tasks[task](what)
-    for task, what in TAIL:
-        tasks[task](what)
+
+    tasks = {
+        EXCHANGE: exchange, RING: ring_step, SPREAD: spread_tables, PLACE: late_places,
+        PICK: listed_sum, LIST: list_step,
+        MASK: make_mask, FINISH: finish, OVER_X: over_x, GATHER: gather, DECODE: decode, LAST: last,
+    }
+    for task, *what in PROGRAM:
+        tasks[task](*what)
 
     pltpu.make_async_copy(res, residual.at[0], res_sem).wait()
     pltpu.make_async_copy(upd, update.at[:, z], upd_sem).wait()
     sent(stage, pair_send)
+    sent(tiles, tile_send)
     for direction in (0, 1):
         sent(ring.at[direction], ring_send.at[direction])
+        sent(brought.at[direction], list_send.at[direction])
     sent(zbuf, z_send)
     sent(xbuf.at[:, pl.ds(0, NX - 1)], x_send)
     for unit in range(len(UNITS)):
@@ -356,6 +531,12 @@
             pltpu.VMEM((2, 2 * SPAN, 2 * SPAN), F32),
             pltpu.VMEM((2, SPAN, 3 * SPAN), BF16),
             pltpu.VMEM((2, 6 * SPAN, 2 * SPAN), BF16),
+            pltpu.VMEM((GRID, 128), F32),
+            pltpu.VMEM((NY - 1, GRID, 128), F32),
+            pltpu.VMEM((2, 128, WIDTH), BF16),
+            pltpu.VMEM((CHUNKS - ROW0, KMAX, COLS), F32),
+            pltpu.VMEM((NY, LISTED, 128), F32),
+            pltpu.VMEM((2, STEPS, HALF_LISTED, 128), F32),
             pltpu.VMEM((CHUNKS, NY, SPAN, COLS), F32),
             pltpu.VMEM((CHUNKS, NY, SPAN, COLS), F32),
             pltpu.VMEM((2, CHUNKS, 2, HALF, COLS), F32),
@@ -373,6 +554,10 @@
             dma((CHUNKS, NY)),
             dma((2,)),
             dma((2, len(UNITS), STEPS)),
+            dma,
+            dma,
+            dma((2,)),
+            dma((2, STEPS)),
             dma,
             dma((len(UNITS),)),
             dma,

time: 64.1 us -> 59 us (0.920)
  the two profiles are of different devices: /device:TPU:24 before, /device:TPU:2 now
where the time goes in v3:
time: 59 us; the launch traced here: 58.8 us
  Pallas kernels  56.7 us (96%)
  local copies, waits for them, and re-layouts  1.49 us (3%)
  between operations  0.64 us (1%)
    pallas_call x1, Pallas kernels, shards(): pl.pallas_call(kernel, out_shape=(pltpu.VMEM((CHUNKS, NZ, PIECE, COLS), F...  56.7 us
    unnamed x2, local copies, waits for them, and re-layouts  1.49 us

profile of v3, /device:TPU:2, one launch (start us, length us, event | category | flops | bytes accessed | tf_op | source)
XLA Modules:
  0.0 58.8 jit_solution(4768477408976185039)
XLA Ops:
  0.6 56.7 %shard_map.68 = (f32[4,8,8,384]{3,2,1,0:T(8,128)S(1)}, f32[1,256,384]{2,1,0:T(8,128)S(1)}) custom-call(bf16[1,1,256,6144]{3,2,1,0:T(8,128)(2,1)} %grad.1, f32[1,256,384]{2,1,0:T(8,128)} %momentum.1, s32[1,4,6]{2,1,0:T(4,128)} %counts.1, s32[1,6,4,16]{3,2,1,0:T(4,128)} %bitcast.3, f32[2,128,128]{2,1,0:T(8,128)} %constant.2.clone.tables), custom_call_target="tpu_custom_call" | custom-call | flops 1000000000 | bytes 5000000 | tf_op jit(solution)/shard_map/pallas_call | solution.py:518
  57.3 0.7 %copy.9 = f32[256,384]{1,0:T(8,128)} copy(f32[256,384]{1,0:T(8,128)S(1)} %bitcast.2) | data formatting | bytes 786432
  58.1 0.7 %copy.10 = f32[1,256,384]{2,1,0:T(8,128)} copy(f32[1,256,384]{2,1,0:T(8,128)S(1)} %get-tuple-element.7) | data formatting | bytes 786432

commit v4 on v3

--- a/solution.py
+++ b/solution.py
@@ -27,7 +27,7 @@
 SLOT = {d: i for i, d in enumerate(DISTANCES)}
 HIGHEST = lax.Precision.HIGHEST
 VMEM_LIMIT = 62 * 2**20
-UNITS = ((0, 0, 3), (1, 0, 3), (2, 0, 3), (3, 0, 3))
+UNITS = ((0, 0, 3), (1, 0, 2), (1, 2, 3), (2, 0, 3), (3, 0, 3))
 GROUPS = ((2, 0), (2, 1), (2, 2), (3, 0), (3, 1), (3, 2))
 NG = len(GROUPS)
 SKIP = 2 * GROUPS[0][1]
@@ -35,20 +35,20 @@
 LISTED = 2 * NG * GRID
 HALF_LISTED = LISTED // 2
 ROW0 = GROUPS[0][0]
-EARLY = tuple(u for u in range(len(UNITS)) if UNITS[u][0] < ROW0)
 LATE = tuple(u for u in range(len(UNITS)) if UNITS[u][0] >= ROW0)
 EXCHANGE, RING, SPREAD, PLACE, PICK, LIST, MASK, FINISH, OVER_X, GATHER, DECODE, LAST = range(12)
 PROGRAM = (
-    [(RING, 0, 0), (EXCHANGE, 0, 4, 8), (RING, 0, 1), (EXCHANGE, 1, 0, 8), (RING, 1, 0), (RING, 1, 1)]
-    + [(EXCHANGE, 3, 0, 8), (EXCHANGE, 2, 0, 8), (SPREAD,), (RING, 0, 2), (PICK, 4), (RING, 0, 3)]
-    + [(LIST, 0), (PICK, 3), (PICK, -3), (RING, 1, 2), (LIST, 1), (RING, 0, 4), (RING, 0, 5)]
-    + [(LIST, 2), (RING, 1, 3), (PICK, 2), (PICK, -2), (LIST, 3), (RING, 0, 6), (PICK, 1), (LIST, 4)]
-    + [(PICK, -1), (RING, 1, 4), (LIST, 5), (MASK, 0), (RING, 1, 5), (FINISH, 0), (LIST, 6)]
-    + [(RING, 1, 6), (RING, 2, 0), (RING, 3, 0), (RING, 2, 1), (RING, 3, 1), (PICK, 0), (PLACE,)]
-    + [(DECODE,), (MASK, 1), (FINISH, 1), (RING, 2, 2), (RING, 3, 2), (OVER_X, 0), (RING, 2, 3)]
-    + [(RING, 3, 3), (RING, 2, 4), (GATHER, 0), (RING, 3, 4), (OVER_X, 2), (RING, 2, 5)]
-    + [(OVER_X, 3), (RING, 3, 5), (RING, 2, 6), (GATHER, 2), (OVER_X, 1), (RING, 3, 6)]
-    + [(GATHER, 3), (LAST, 2), (GATHER, 1), (LAST, 3)]
+    [(RING, 0, 0), (EXCHANGE, 0, 3, 8), (RING, 0, 1), (EXCHANGE, 1, 0, 8), (RING, 1, 0), (RING, 1, 1)]
+    + [(RING, 2, 0), (RING, 2, 1), (EXCHANGE, 3, 0, 8), (EXCHANGE, 2, 0, 8), (SPREAD,), (RING, 0, 2)]
+    + [(PICK, 4), (RING, 0, 3), (LIST, 0), (PICK, 3), (PICK, -3), (LIST, 1), (LIST, 2), (RING, 0, 4)]
+    + [(RING, 0, 5), (RING, 1, 2), (PICK, 2), (PICK, -2), (LIST, 3), (LIST, 4), (RING, 0, 6)]
+    + [(RING, 1, 3), (RING, 2, 2), (PICK, 1), (PICK, -1), (LIST, 5), (LIST, 6), (RING, 2, 3)]
+    + [(MASK, 0), (RING, 1, 4), (FINISH, 0), (RING, 1, 5), (RING, 2, 4), (RING, 3, 0), (PICK, 0), (PLACE,)]
+    + [(DECODE,), (RING, 4, 0), (RING, 1, 6), (RING, 2, 5), (RING, 2, 6), (RING, 3, 1), (RING, 4, 1)]
+    + [(MASK, 1), (RING, 3, 2), (RING, 4, 2), (FINISH, 1), (FINISH, 2), (OVER_X, 0), (RING, 3, 3)]
+    + [(RING, 4, 3), (OVER_X, 3), (RING, 3, 4), (RING, 4, 4), (OVER_X, 4), (GATHER, 0), (RING, 3, 5)]
+    + [(RING, 4, 5), (GATHER, 3), (OVER_X, 1), (OVER_X, 2), (RING, 3, 6), (RING, 4, 6)]
+    + [(GATHER, 4), (GATHER, 1), (GATHER, 2), (LAST, 3), (LAST, 4)]
 )
 
 
@@ -104,11 +104,15 @@
         return {"rep": z * NX + lax.rem(x + d, NX)}
 
     partners = (
-        [peer]
-        + [at_y(d) for d in range(1, NY)]
-        + [at_z(d) for d in range(1, NZ)]
-        + [at_x(d) for d in range(1, NX)]
+        [at_z(d) for d in (4, 3, 5, 2, 6, 1, 7)]
+        + [at_x(d) for d in (2, 1, 3)]
+        + [at_y(d) for d in (4, 3, 5, 2, 6, 1, 7)]
+        + [peer]
     )
+
+    barrier = pltpu.get_barrier_semaphore()
+    for partner in partners:
+        pl.semaphore_signal(barrier, inc=1, device_id=partner, device_id_type=MESH)
 
     small = [
         (counts.at[0], cnt_v), (blocks.at[0], blk_v),
@@ -125,12 +129,8 @@
         pltpu.make_async_copy(src, dst, load_sem.at[CHUNKS + i])
         for i, (src, dst) in enumerate(small)
     ]
-    for load in loads:
-        load.start()
-
-    barrier = pltpu.get_barrier_semaphore()
-    for partner in partners:
-        pl.semaphore_signal(barrier, inc=1, device_id=partner, device_id_type=MESH)
+    for i in (0, CHUNKS + 1, 1, CHUNKS, CHUNKS + 2, CHUNKS + 3, 3, 2):
+        loads[i].start()
 
     def columns(distance, which, first_lane=0, width=COLS):
         target = lax.rem(y + distance + NY, NY) * NCORE + which
@@ -306,22 +306,27 @@
         return pl.ds(half * HALF_LISTED, HALF_LISTED)
 
     def list_copy(direction, step):
-        if step < 2:
+        if step < 3:
             distance, half = step_distance(direction, step)
             source = packed.at[SLOT[4 if distance == -4 else distance], half_rows(half)]
         else:
             source = brought.at[direction, step - 2]
         return moved(
             source, brought.at[direction, step],
-            list_send.at[direction], list_recv.at[direction, step], neighbours[direction],
+            list_send.at[direction], list_recv.at[direction, step],
+            at_y((2, NY - 2)[direction]) if step == 0 else neighbours[direction],
         )
 
     def list_step(step):
         for direction in (0, 1):
             distance, half = step_distance(direction, step)
-            if step >= 2:
+            if step >= 3:
                 list_copy(direction, step - 2).wait_recv()
-                brought[direction, step - 2] += packed[SLOT[distance], half_rows(half)]
+                more = packed[SLOT[distance], half_rows(half)]
+                if step == 4:
+                    list_copy(direction, 0).wait_recv()
+                    more = more + brought[direction, 0]
+                brought[direction, step - 2] += more
             list_copy(direction, step).start()
 
     def decode():
@@ -458,13 +463,16 @@
         update_copy(unit).start()
 
     def exchange(k, begin, end):
-        if k > 1:
+        if k > 0:
+            loads[k].wait()
             for i in range(begin, end):
                 fill_stage(k, i)
         for i in range(begin, end):
             pair_copy(k, i).start()
 
     def spread_tables():
+        for i in (CHUNKS, CHUNKS + 2, CHUNKS + 3):
+            loads[i].wait()
         for way in range(2):
             left_v[way] = split_table(tab_v[1 - way, :SPAN, :SPAN], 1)
             right_v[way] = split_table(tab_v[way], 0)
@@ -475,19 +483,15 @@
         for k in range(ROW0, CHUNKS):
             place_v[k - ROW0] = places(k)
 
-    for load in loads[CHUNKS : CHUNKS + 2]:
-        load.wait()
+    loads[0].wait()
+    for i in range(NY):
+        fill_stage(0, i)
+    loads[CHUNKS + 1].wait()
     make_tile()
-    for k in range(2):
-        loads[k].wait()
-        for i in range(NY):
-            fill_stage(k, i)
     pl.semaphore_wait(barrier, len(partners))
-    exchange(0, 0, 4)
+    exchange(0, 0, 3)
     for d in (4, 3, 5, 2, 6, 1, 7):
         tile_copy(d).start()
-    for load in loads[2:CHUNKS] + loads[CHUNKS + 2 :]:
-        load.wait()
 
     tasks = {
         EXCHANGE: exchange, RING: ring_step, SPREAD: spread_tables, PLACE: late_places,
@@ -509,6 +513,17 @@
     for unit in range(len(UNITS)):
         arrived(zbuf.at[UNITS[unit][0], :, :, lanes(unit)], a_recv.at[unit])
     sent(zbuf, a_send)
+
+
+def put_out(update, residual, update_out, residual_out, sems):
+    copies = [
+        pltpu.make_async_copy(update, update_out, sems.at[0]),
+        pltpu.make_async_copy(residual, residual_out, sems.at[1]),
+    ]
+    for copy in copies:
+        copy.start()
+    for copy in copies:
+        copy.wait()
 
 
 def shards(grad_parts, momentum, keep_counts, keep_blocks):
@@ -572,7 +587,16 @@
             flops=10**9, bytes_accessed=5 * 10**6, transcendentals=0
         ),
     )(grad_parts, momentum, keep_counts, keep_blocks.transpose(0, 2, 1, 3), jnp.asarray(dct_tables()))
-    return update.reshape(ROWS, COLS), residual
+    return pl.pallas_call(
+        put_out,
+        out_shape=(
+            jax.ShapeDtypeStruct((ROWS, COLS), F32),
+            jax.ShapeDtypeStruct((1, ROWS, COLS), F32),
+        ),
+        in_specs=[anywhere] * 2,
+        out_specs=(anywhere, anywhere),
+        scratch_shapes=[dma((2,))],
+    )(update.reshape(ROWS, COLS), residual)
 
 
 def solution(mesh):

time: 59 us -> 83.3 us (1.41)
  Pallas kernels: 56.7 us -> 81.1 us
    pallas_call x0 -> x1, Pallas kernels: none -> 24.9 us  [shards(): pl.pallas_call(put_out, out_shape=(jax.ShapeDtypeStruct((ROWS, COLS), F32...]
where the time goes in v4:
time: 83.3 us; the launch traced here: 83.2 us
  Pallas kernels  81.1 us (97%)
  local copies, waits for them, and re-layouts  1.5 us (2%)
    pallas_call x1, Pallas kernels, shards(): pl.pallas_call(kernel, out_shape=(pltpu.VMEM((CHUNKS, NZ, PIECE, COLS), F...  56.1 us
    pallas_call x1, Pallas kernels, shards(): pl.pallas_call(put_out, out_shape=(jax.ShapeDtypeStruct((ROWS, COLS), F32...  24.9 us

profile of v4, /device:TPU:2, one launch (start us, length us, event | category | flops | bytes accessed | tf_op | source)
XLA Modules:
  0.0 83.2 jit_solution(10660143356369483995)
XLA Ops:
  0.6 56.1 %shard_map.68 = (f32[4,8,8,384]{3,2,1,0:T(8,128)S(1)}, f32[1,256,384]{2,1,0:T(8,128)S(1)}) custom-call(bf16[1,1,256,6144]{3,2,1,0:T(8,128)(2,1)} %grad.1, f32[1,256,384]{2,1,0:T(8,128)} %momentum.1, s32[1,4,6]{2,1,0:T(4,128)} %counts.1, s32[1,6,4,16]{3,2,1,0:T(4,128)} %bitcast.3, f32[2,128,128]{2,1,0:T(8,128)} %constant.2.clone.tables), custom_call_target="tpu_custom_call" | custom-call | flops 1000000000 | bytes 5000000 | tf_op jit(solution)/shard_map/pallas_call | solution.py:533
  56.8 0.0 copy-start
  56.8 0.7 copy-done
  57.5 0.0 copy-start.1
  57.5 0.7 copy-done.1
  58.3 24.9 %shard_map.69 = (f32[256,384]{1,0:T(8,128)}, f32[1,256,384]{2,1,0:T(8,128)}) custom-call(f32[256,384]{1,0:T(8,128)} %bitcast.2, f32[1,256,384]{2,1,0:T(8,128)} %copy-done.1), custom_call_target="tpu_custom_call" | custom-call | tf_op jit(solution)/shard_map/pallas_call | solution.py:590
Async XLA Ops:
  56.8 0.8 copy-start
  57.5 0.7 copy-start.1

commit v5 on v4

--- a/solution.py
+++ b/solution.py
@@ -515,17 +515,6 @@
     sent(zbuf, a_send)
 
 
-def put_out(update, residual, update_out, residual_out, sems):
-    copies = [
-        pltpu.make_async_copy(update, update_out, sems.at[0]),
-        pltpu.make_async_copy(residual, residual_out, sems.at[1]),
-    ]
-    for copy in copies:
-        copy.start()
-    for copy in copies:
-        copy.wait()
-
-
 def shards(grad_parts, momentum, keep_counts, keep_blocks):
     anywhere = pl.BlockSpec(memory_space=pl.ANY)
     outside = pl.BlockSpec(memory_space=pltpu.HBM)
@@ -587,16 +576,7 @@
             flops=10**9, bytes_accessed=5 * 10**6, transcendentals=0
         ),
     )(grad_parts, momentum, keep_counts, keep_blocks.transpose(0, 2, 1, 3), jnp.asarray(dct_tables()))
-    return pl.pallas_call(
-        put_out,
-        out_shape=(
-            jax.ShapeDtypeStruct((ROWS, COLS), F32),
-            jax.ShapeDtypeStruct((1, ROWS, COLS), F32),
-        ),
-        in_specs=[anywhere] * 2,
-        out_specs=(anywhere, anywhere),
-        scratch_shapes=[dma((2,))],
-    )(update.reshape(ROWS, COLS), residual)
+    return update.reshape(ROWS, COLS), residual
 
 
 def solution(mesh):

time: 83.3 us -> 58.4 us (0.70)
  Pallas kernels: 81.1 us -> 56.1 us
    pallas_call x1 -> x0, Pallas kernels: 24.9 us -> none  [shards(): pl.pallas_call(put_out, out_shape=(jax.ShapeDtypeStruct((ROWS, COLS), F32...]
where the time goes in v5:
time: 58.4 us; the launch traced here: 58.3 us
  Pallas kernels  56.1 us (96%)
  local copies, waits for them, and re-layouts  1.49 us (3%)
  between operations  0.64 us (1%)
    pallas_call x1, Pallas kernels, shards(): pl.pallas_call(kernel, out_shape=(pltpu.VMEM((CHUNKS, NZ, PIECE, COLS), F...  56.1 us
    unnamed x2, local copies, waits for them, and re-layouts  1.49 us

profile of v5, /device:TPU:2, one launch (start us, length us, event | category | flops | bytes accessed | tf_op | source)
XLA Modules:
  0.0 58.3 jit_solution(13844730059440373556)
XLA Ops:
  0.6 56.1 %shard_map.68 = (f32[4,8,8,384]{3,2,1,0:T(8,128)S(1)}, f32[1,256,384]{2,1,0:T(8,128)S(1)}) custom-call(bf16[1,1,256,6144]{3,2,1,0:T(8,128)(2,1)} %grad.1, f32[1,256,384]{2,1,0:T(8,128)} %momentum.1, s32[1,4,6]{2,1,0:T(4,128)} %counts.1, s32[1,6,4,16]{3,2,1,0:T(4,128)} %bitcast.3, f32[2,128,128]{2,1,0:T(8,128)} %constant.2.clone.tables), custom_call_target="tpu_custom_call" | custom-call | flops 1000000000 | bytes 5000000 | tf_op jit(solution)/shard_map/pallas_call | solution.py:522
  56.8 0.7 %copy.9 = f32[256,384]{1,0:T(8,128)} copy(f32[256,384]{1,0:T(8,128)S(1)} %bitcast.2) | data formatting | bytes 786432
  57.5 0.7 %copy.10 = f32[1,256,384]{2,1,0:T(8,128)} copy(f32[1,256,384]{2,1,0:T(8,128)S(1)} %get-tuple-element.7) | data formatting | bytes 786432
